TPU v7x, 512 devices: a whole 4x8x8 slice. The times are simulated.
512 devices in a mesh: tm: 64 (over x, z, core), region: 8 (over y).
Axes of the slice: x: 4, y: 8, z: 8, core: 2. Of those that a mesh axis runs over, the one named last changes fastest.
Arguments:
- activity: bfloat16 [6144, 131072], P('region', 'tm'), may hold values from -6 to 6
- test_matrix: bfloat16 [131072, 512], P('tm', 'region'), may hold values from -0.015625 to 0.015625
- basis_mix: float32 [512, 64], replicated, may hold values from -0.25 to 0.25
- recurrent: float32 [64, 64], replicated, may hold values from -0.75 to 0.75
- latent_bias: float32 [64], replicated, may hold values from -2 to 2
- readout: bfloat16 [6144, 64], P('region'), may hold values from -0.75 to 0.75
- region_in: bfloat16 [6144, 8], P('region'), may hold values from -0.21875 to 0.21875
- region_out: bfloat16 [6144, 8], P('region'), may hold values from -1 to 1
- region_of_block: int32 [48], replicated, may hold values from 0 to 7, never falling along the last dimension, each value on 1 to 12 neighbouring positions
- region_mask: int32 [8, 8], replicated, may hold values 0 or 1
Outputs:
- latents: float32 [64, 131072], P(None, 'tm')
- frame_loss: float32 [131072], P('tm')
- readout_score: float32 [6144, 64], P('region')
Inputs may be any that keep to these rules, and one draw needn't show every extreme that they name: `region_of_block`: blocks of one region are consecutive, every region holds at least one block, and no region holds more than 12 blocks.
All inputs are finite; a program needn't handle non-finite values.
Results may differ from a plain program's by a relative error of at most 0.0028.
Values may be sent and summed in bfloat16 or wider, within the bound.
No kernel may reach another device: no remote copies, remote signals or barrier semaphores. Data moves between devices by JAX's collectives and lax.ppermute only.
A program may use at most 64 MiB of HBM per device.

v0:
```python
import jax
import jax.numpy as jnp
from jax import lax
from jax.sharding import PartitionSpec as P

BLOCK = 128
precise = lax.Precision.HIGHEST
epsilon = 1e-05


def from_behind(block, axis, distance):
    devices = range(lax.axis_size(axis))
    route = [(i - distance, i) for i in devices if i - distance in devices]
    return lax.ppermute(block, axis, route)


def orthonormal(sketch, gram):
    lower = jnp.linalg.cholesky(gram)
    return jax.scipy.linalg.solve_triangular(lower, sketch.T, lower=True).T


def region_tables(block_regions, region_mask, region_in, region_out):
    regions = region_mask.shape[0]
    signal_width = region_in.shape[1]
    block_total = block_regions.shape[0]
    block_rows = region_in.shape[0] // block_total
    onehot = (block_regions[:, None] == jnp.arange(regions, dtype=jnp.int32)[None, :]).astype(
        jnp.float32
    )
    onehot = jnp.broadcast_to(onehot[:, None, :], (block_total, block_rows, regions)).reshape(
        block_total * block_rows, regions
    )
    allowed = jnp.dot(onehot, region_mask.astype(jnp.float32), precision=precise)
    region_feed = (onehot[:, :, None] * region_in.astype(jnp.float32)[:, None, :]).reshape(
        -1, regions * signal_width
    )
    spread = (allowed[:, :, None] * region_out.astype(jnp.float32)[:, None, :]).reshape(
        -1, regions * signal_width
    )
    return (region_feed.astype(jnp.bfloat16), spread.astype(jnp.bfloat16))


def local(
    activity,
    test_matrix,
    basis_mix,
    recurrent,
    latent_bias,
    readout,
    region_in,
    region_out,
    region_of_block,
    region_mask,
):
    neurons_here, frames_here = activity.shape
    contract = (((0,), (0,)), ((), ()))
    block_count = neurons_here // BLOCK
    my_blocks = lax.dynamic_slice_in_dim(
        region_of_block, lax.axis_index("region") * block_count, block_count
    )
    region_feed, spread = region_tables(my_blocks, region_mask, region_in, region_out)
    test_full = lax.all_gather(test_matrix, "region", axis=1, tiled=True)
    sketch_rows = lax.psum_scatter(
        jnp.dot(activity, test_full, preferred_element_type=jnp.float32),
        "tm",
        scatter_dimension=0,
        tiled=True,
    )
    gram = lax.psum(jnp.dot(sketch_rows.T, sketch_rows, precision=precise), ("tm", "region"))
    loading_rows = jnp.dot(orthonormal(sketch_rows, gram), basis_mix, precision=precise).astype(
        jnp.bfloat16
    )
    latent_part = lax.dot_general(
        lax.all_gather(loading_rows, "tm", axis=0, tiled=True),
        activity,
        contract,
        preferred_element_type=jnp.float32,
    )
    signal_part = lax.dot_general(
        region_feed, activity, contract, preferred_element_type=jnp.float32
    )
    latents, signals = lax.psum((latent_part, signal_part), "region")
    prior_latent, prior_signal = from_behind((latents[:, -1:], signals[:, -1:]), "tm", 1)
    lagged_latents = jnp.concatenate([prior_latent, latents[:, :-1]], axis=1)
    lagged_signals = jnp.concatenate([prior_signal, signals[:, :-1]], axis=1)
    hidden = jnp.tanh(jnp.dot(recurrent, lagged_latents, precision=precise) + latent_bias[:, None])
    predicted = jnp.dot(readout, hidden.astype(jnp.bfloat16), preferred_element_type=jnp.float32)
    predicted = predicted + jnp.dot(
        spread, lagged_signals.astype(jnp.bfloat16), preferred_element_type=jnp.float32
    )
    error = activity.astype(jnp.float32) - predicted
    squared = error * error
    cross, error_sq, hidden_sq = lax.psum(
        (
            jnp.dot(error, hidden.T, precision=precise),
            jnp.sum(squared, axis=1),
            jnp.sum(hidden * hidden, axis=1),
        ),
        "tm",
    )
    frame_sq = lax.psum(jnp.sum(squared, axis=0), "region")
    frames_all = frames_here * lax.axis_size("tm")
    frame_loss = frame_sq / (neurons_here * lax.axis_size("region"))
    readout_score = cross / jnp.sqrt(
        frames_all
        * (error_sq[:, None] / frames_all + epsilon)
        * (hidden_sq[None, :] / frames_all + epsilon)
    )
    return (latents, frame_loss, readout_score)


def solution(mesh):
    in_specs = (
        P("region", "tm"),
        P("tm", "region"),
        P(),
        P(),
        P(),
        P("region", None),
        P("region", None),
        P("region", None),
        P(),
        P(),
    )
    out_specs = (P(None, "tm"), P("tm"), P("region", None))
    return jax.shard_map(local, mesh=mesh, in_specs=in_specs, out_specs=out_specs, check_vma=False)
```

profile of v0, /device:TPU:8, one launch (start us, length us, event | category | flops | bytes accessed | tf_op | source)
XLA Modules:
  0.0 1049.4 jit_solution(13345600834286897948)
XLA Ops:
  8.0 50.1 %all-gather.3.cloned.1.call-done = bf16[2048,512]{0,1:T(8,128)(2,1)} async-done(((bf16[2048,64]{0,1:T(8,128)(2,1)}), bf16[2048,512]{0,1:T(8,128)(2,1)}) %all-gather.3.cloned.1.call-update) | async-done | bytes 2097168 | tf_op jit(solution)/shard_map/all_gather | solution.py:62
  58.1 5.5 fusion.73
  63.6 141.2 %fusion = f32[16,512]{1,0:T(8,128)S(1)} fusion(f32[768,512]{1,0:T(8,128)} %fusion.73), kind=kCustom, calls=%all-reduce-scatter | all-reduce-scatter fusion | flops 524289 | bytes 1607680
  212.7 11.6 %collective-permute-start.11 = (f32[16,512]{1,0:T(8,128)S(1)}, f32[16,512]{1,0:T(8,128)S(1)}, u32[]{:S(2)}, u32[]{:S(2)}) collective-permute-start(f32[16,512]{1,0:T(8,128)S(1)} %fusion), channel_id=1, source_target_pairs={{0,80},{8,88},{16,96},{24,104},{32,112},{40,120},{48,128},{56,136}... | collective-permute-start | bytes 98312
  224.3 1.9 collective-permute-start.10
  226.3 5.7 collective-permute-start.9
  233.4 3.8 collective-permute-start.7
  237.3 4.1 collective-permute-start.6
  241.5 3.3 collective-permute-start.5
  244.8 2.7 collective-permute-start.4
  247.5 2.5 collective-permute-start.3
  250.1 2.0 collective-permute-start.2
  254.9 23.2 %concatenate.21 = f32[268,512]{1,0:T(8,128)} concatenate(f32[12,512]{1,0:T(8,128)S(1)} %collective-permute-done.17, f32[16,512]{1,0:T(8,128)S(1)} %collective-permute-done.16, f32[16,512]{1,0:T(8,128)S(1)} %collective-permute-done.15, f32[16,512]{1,0:T(8,128)S(1)} %collective-permute-done.14, f32[16,512]{1,0:T(8,128)S(1)} %collective-permute-done.13, ...), dimensions={0} | concatenate | bytes 1097728
  278.1 2.9 fusion.50
  281.6 1.5 fusion.26
  284.4 262.1 %all-reduce.9.cloned.1.call-done = f32[512,512]{0,1:T(8,128)} async-done(((f32[512,512]{0,1:T(8,128)}), f32[512,512]{0,1:T(8,128)}) %all-reduce.9.cloned.1.call-update) | async-done | bytes 1048592 | tf_op jit(solution)/shard_map/psum | solution.py:69
  546.5 2.6 copy.25
  549.1 1.8 fusion.4
  551.8 11.7 %cholesky.104 = f32[128,128]{1,0:T(8,128)S(1)} custom-call(f32[128,128]{1,0:T(8,128)S(1)} %cholesky.266), custom_call_target="Cholesky" | custom-call | tf_op jit(solution)/shard_map/jit(cholesky)/cholesky | solution.py:18
  563.6 9.8 custom-call.31
  574.5 1.9 constant_dynamic-update-slice_fusion.3
  578.4 12.5 %cholesky.217 = f32[128,128]{1,0:T(8,128)S(1)} custom-call(f32[128,128]{1,0:T(8,128)} %cholesky.270), custom_call_target="Cholesky" | custom-call | tf_op jit(solution)/shard_map/jit(cholesky)/cholesky | solution.py:18
  591.6 10.8 %custom-call.32 = f32[1,128,128]{1,2,0:T(8,128)S(1)} custom-call(f32[1,128,128]{2,1,0:T(8,128)} %get-tuple-element.31), custom_call_target="InvertDiagBlocksLowerTriangular" | custom-call | tf_op jit(solution)/shard_map/jit(cholesky)/cholesky | solution.py:18
  604.8 11.7 %cholesky.238 = f32[128,128]{1,0:T(8,128)S(1)} custom-call(f32[128,128]{1,0:T(8,128)S(1)} %cholesky.275), custom_call_target="Cholesky" | custom-call | tf_op jit(solution)/shard_map/jit(cholesky)/cholesky | solution.py:18
  617.8 9.8 custom-call.33
  629.9 11.9 %cholesky.255 = f32[128,128]{1,0:T(8,128)S(1)} custom-call(f32[128,128]{1,0:T(8,128)S(1)} %convolution_subtract_fusion.2), custom_call_target="Cholesky" | custom-call | tf_op jit(solution)/shard_map/jit(cholesky)/cholesky | solution.py:18
  646.3 2.3 select_select_fusion
  648.6 14.4 %while.1 = (s32[]{:T(128)}, f32[512,512]{1,0:T(8,128)}, s32[4,2]{0,1:T(2,128)S(1)}, f32[4,128,128]{2,1,0:T(8,128)}, s32[]{:T(128)}) while((s32[]{:T(128)}, f32[512,512]{1,0:T(8,128)}, s32[4,2]{0,1:T(2,128)S(1)}, f32[4,128,128]{2,1,0:T(8,128)}, s32[]{:T(128)}) %tuple.34), condition=%wide.while_cond, body=%wide.while_body.sunk | while | flops 2 | bytes 132205 | solution.py:19
  649.3 3.0 bitcast_dynamic-update-slice_fusion.2
  652.9 3.0 bitcast_dynamic-update-slice_fusion.2
  656.5 3.0 bitcast_dynamic-update-slice_fusion.2
  660.1 2.9 bitcast_dynamic-update-slice_fusion.2
  663.0 40.1 %custom-call.34 = f32[4,128,128]{1,2,0:T(8,128)S(1)} custom-call(f32[4,128,128]{2,1,0:T(8,128)} %get-tuple-element.10), custom_call_target="InvertDiagBlocksLowerTriangular" | custom-call | tf_op jit(solution)/shard_map/jit(_solve_triangular)/triangular_solve | solution.py:19
  710.3 43.1 %all-gather = bf16[64,12,64]{2,1,0:T(8,128)(2,1)S(1)} all-gather(bf16[1,12,64]{2,1,0:T(8,128)(2,1)S(1)} %fusion.3), channel_id=1, replica_groups=mesh['tm'=64,'region'=8] {'tm'}, dimensions={0}, use_global_device_ids=true | all-gather | bytes 99840 | tf_op jit(solution)/shard_map/all_gather | solution.py:74
  754.2 2.4 fusion.74
  756.7 35.5 %all-reduce.14 = bf16[64,2048]{1,0:T(8,128)(2,1)S(1)} all-reduce(f32[64,2048]{1,0:T(8,128)} %fusion.26), channel_id=1, replica_groups=mesh['tm'=64,'region'=8] {'region'}, use_global_device_ids=true, to_apply=%region_11.12 | all-reduce | flops 131072 | bytes 786432 | tf_op jit(solution)/shard_map/psum | solution.py:82
  792.8 1.9 collective-permute-start.1
  794.7 36.6 %all-reduce.11.cloned.1.call-done = f32[64,2048]{1,0:T(8,128)} async-done(((f32[64,2048]{1,0:T(8,128)}), f32[64,2048]{1,0:T(8,128)}) %all-reduce.11.cloned.1.call-update) | async-done | bytes 524304 | tf_op jit(solution)/shard_map/psum | solution.py:82
  832.7 2.1 collective-permute-start
  835.7 2.8 copy.26
  838.6 1.9 multiply_reduce_fusion.2
  840.5 2.1 fusion.12
  842.6 2.5 multiply_reduce_fusion
  845.2 4.8 fusion.75
  850.0 129.4 %all-reduce.3 = (f32[64]{0:T(128)S(1)}, f32[768]{0:T(1024)S(1)}) all-reduce(f32[64]{0:T(128)S(1)} %get-tuple-element.38, f32[768]{0:T(1024)S(1)} %get-tuple-element.11), channel_id=1, replica_groups=mesh['tm'=64,'region'=8] {'tm'}, use_global_device_ids=true, to_apply=%region_18.19 | all-reduce | flops 832 | bytes 6656 | tf_op jit(solution)/shard_map/psum | solution.py:93
  979.4 15.0 %psum.52 = f32[2048]{0:T(1024)S(1)} all-reduce(f32[2048]{0:T(1024)S(1)} %get-tuple-element.12), channel_id=1, replica_groups=mesh['tm'=64,'region'=8] {'region'}, use_global_device_ids=true, to_apply=%region_13.14 | all-reduce | flops 2048 | bytes 16384 | tf_op jit(solution)/shard_map/psum | solution.py:101
  995.0 45.1 %all-reduce.13.cloned.1.call-done = f32[768,64]{0,1:T(8,128)} async-done(((f32[768,64]{0,1:T(8,128)}), f32[768,64]{0,1:T(8,128)}) %all-reduce.13.cloned.1.call-update) | async-done | bytes 196624 | tf_op jit(solution)/shard_map/psum | solution.py:93
  1040.1 1.7 rsqrt_multiply_fusion
  (118 shorter events, 41.8 us)
Async XLA Ops:
  7.2 702.9 %copy-start = (f32[512,64]{0,1:T(8,128)S(1)}, f32[512,64]{0,1:T(8,128)}, u32[]{:S(2)}) copy-start(f32[512,64]{0,1:T(8,128)} %param.12) | copy-start | bytes 393220
  7.2 50.9 %all-gather.3.cloned.1.call-start = ((), (), s32[]{:S(2)}) async-start(), calls=%async_computation | async-start | bytes 2359296 | tf_op jit(solution)/shard_map/all_gather | solution.py:62
  7.9 204.7 %copy-start.16 = (s32[48]{0:T(128)S(1)}, s32[48]{0:T(128)}, u32[]{:S(2)}) copy-start(s32[48]{0:T(128)} %param.18) | copy-start | bytes 580
  7.9 538.6 %all-reduce.9.cloned.1.call-start = ((), (), s32[]{:S(2)}) async-start(), calls=%async_computation.1 | async-start | bytes 2097152 | tf_op jit(solution)/shard_map/psum | solution.py:69
  63.6 218.0 %copy-start.1 = (bf16[768,2048]{1,0:T(8,128)(2,1)S(1)}, bf16[768,2048]{1,0:T(8,128)(2,1)}, u32[]{:S(2)}) copy-start(bf16[768,2048]{1,0:T(8,128)(2,1)} %param.10) | copy-start | bytes 9437188
  204.8 6.5 collective-permute-start.17
  206.1 6.6 collective-permute-start.16
  207.4 16.9 %collective-permute-start.15 = (f32[16,512]{1,0:T(8,128)S(1)}, f32[16,512]{1,0:T(8,128)S(1)}, u32[]{:S(2)}, u32[]{:S(2)}) collective-permute-start(f32[16,512]{1,0:T(8,128)S(1)} %fusion), channel_id=1, source_target_pairs={{0,112},{8,120},{16,128},{24,136},{32,144},{40,152},{48,160},{56,1... | collective-permute-start | bytes 98312
  208.7 17.5 %collective-permute-start.14 = (f32[16,512]{1,0:T(8,128)S(1)}, f32[16,512]{1,0:T(8,128)S(1)}, u32[]{:S(2)}, u32[]{:S(2)}) collective-permute-start(f32[16,512]{1,0:T(8,128)S(1)} %fusion), channel_id=1, source_target_pairs={{0,104},{8,112},{16,120},{24,128},{32,136},{40,144},{48,152},{56,1... | collective-permute-start | bytes 98312
  210.0 21.9 %collective-permute-start.13 = (f32[16,512]{1,0:T(8,128)S(1)}, f32[16,512]{1,0:T(8,128)S(1)}, u32[]{:S(2)}, u32[]{:S(2)}) collective-permute-start(f32[16,512]{1,0:T(8,128)S(1)} %fusion), channel_id=1, source_target_pairs={{0,96},{8,104},{16,112},{24,120},{32,128},{40,136},{48,144},{56,15... | collective-permute-start | bytes 98312
  211.3 22.1 %collective-permute-start.12 = (f32[16,512]{1,0:T(8,128)S(1)}, f32[16,512]{1,0:T(8,128)S(1)}, u32[]{:S(2)}, u32[]{:S(2)}) collective-permute-start(f32[16,512]{1,0:T(8,128)S(1)} %fusion), channel_id=1, source_target_pairs={{0,88},{8,96},{16,104},{24,112},{32,120},{40,128},{48,136},{56,144... | collective-permute-start | bytes 98312
  212.7 24.6 %collective-permute-start.11 = (f32[16,512]{1,0:T(8,128)S(1)}, f32[16,512]{1,0:T(8,128)S(1)}, u32[]{:S(2)}, u32[]{:S(2)}) collective-permute-start(f32[16,512]{1,0:T(8,128)S(1)} %fusion), channel_id=1, source_target_pairs={{0,80},{8,88},{16,96},{24,104},{32,112},{40,120},{48,128},{56,136}... | collective-permute-start | bytes 98312
  224.3 17.2 %collective-permute-start.10 = (f32[16,512]{1,0:T(8,128)S(1)}, f32[16,512]{1,0:T(8,128)S(1)}, u32[]{:S(2)}, u32[]{:S(2)}) collective-permute-start(f32[16,512]{1,0:T(8,128)S(1)} %fusion), channel_id=1, source_target_pairs={{0,72},{8,80},{16,88},{24,96},{32,104},{40,112},{48,120},{56,128},... | collective-permute-start | bytes 98312
  226.3 18.6 %collective-permute-start.9 = (f32[16,512]{1,0:T(8,128)S(1)}, f32[16,512]{1,0:T(8,128)S(1)}, u32[]{:S(2)}, u32[]{:S(2)}) collective-permute-start(f32[16,512]{1,0:T(8,128)S(1)} %fusion), channel_id=1, source_target_pairs={{0,64},{8,72},{16,80},{24,88},{32,96},{40,104},{48,112},{56,120},{... | collective-permute-start | bytes 98312
  231.9 15.6 %collective-permute-start.8 = (f32[16,512]{1,0:T(8,128)S(1)}, f32[16,512]{1,0:T(8,128)S(1)}, u32[]{:S(2)}, u32[]{:S(2)}) collective-permute-start(f32[16,512]{1,0:T(8,128)S(1)} %fusion), channel_id=1, source_target_pairs={{0,56},{8,64},{16,72},{24,80},{32,88},{40,96},{48,104},{56,112},{6... | collective-permute-start | bytes 98312
  233.4 16.7 %collective-permute-start.7 = (f32[16,512]{1,0:T(8,128)S(1)}, f32[16,512]{1,0:T(8,128)S(1)}, u32[]{:S(2)}, u32[]{:S(2)}) collective-permute-start(f32[16,512]{1,0:T(8,128)S(1)} %fusion), channel_id=1, source_target_pairs={{0,48},{8,56},{16,64},{24,72},{32,80},{40,88},{48,96},{56,104},{64... | collective-permute-start | bytes 98312
  237.3 14.9 %copy-start.11 = (f32[6,8]{1,0:T(8,128)}, f32[6,8]{1,0:T(8,128)S(1)}, u32[]{:S(2)}) copy-start(f32[6,8]{1,0:T(8,128)S(1)} %fusion.66) | copy-start | bytes 580
  237.3 12.7 %copy-start.5 = (f32[16,512]{1,0:T(8,128)}, f32[16,512]{1,0:T(8,128)S(1)}, u32[]{:S(2)}) copy-start(f32[16,512]{1,0:T(8,128)S(1)} %collective-permute-done.11) | copy-start | bytes 98308
  237.3 17.5 %collective-permute-start.6 = (f32[16,512]{1,0:T(8,128)S(1)}, f32[16,512]{1,0:T(8,128)}, u32[]{:S(2)}, u32[]{:S(2)}) collective-permute-start(f32[16,512]{1,0:T(8,128)S(1)} %fusion), channel_id=1, source_target_pairs={{0,40},{8,48},{16,56},{24,64},{32,72},{40,80},{48,88},{56,96},{64,... | collective-permute-start | bytes 98312
  241.5 10.6 %copy-start.6 = (f32[16,512]{1,0:T(8,128)}, f32[16,512]{1,0:T(8,128)S(1)}, u32[]{:S(2)}) copy-start(f32[16,512]{1,0:T(8,128)S(1)} %collective-permute-done.10) | copy-start | bytes 98308
  241.5 13.4 %collective-permute-start.5 = (f32[16,512]{1,0:T(8,128)S(1)}, f32[16,512]{1,0:T(8,128)}, u32[]{:S(2)}, u32[]{:S(2)}) collective-permute-start(f32[16,512]{1,0:T(8,128)S(1)} %fusion), channel_id=1, source_target_pairs={{0,32},{8,40},{16,48},{24,56},{32,64},{40,72},{48,80},{56,88},{64,... | collective-permute-start | bytes 98312
  244.8 7.4 copy-start.7
  244.8 10.1 collective-permute-start.4
  247.5 4.7 copy-start.8
  247.5 7.4 collective-permute-start.3
  250.1 2.1 copy-start.9
  250.1 4.8 collective-permute-start.2
  281.0 550.3 %all-reduce.11.cloned.1.call-start = ((), (), s32[]{:S(2)}) async-start(), calls=%async_computation.2 | async-start | bytes 1048576 | tf_op jit(solution)/shard_map/psum | solution.py:82
  550.9 1.0 copy-start.3
  709.2 125.7 %copy-start.12 = (f32[6,8]{1,0:T(8,128)S(1)}, f32[6,8]{1,0:T(8,128)}, u32[]{:S(2)}) copy-start(f32[6,8]{1,0:T(8,128)} %copy-done.11) | copy-start | bytes 580
  709.2 125.7 %copy-start.15 = (s32[8,8]{1,0:T(8,128)S(1)}, s32[8,8]{1,0:T(8,128)}, u32[]{:S(2)}) copy-start(s32[8,8]{1,0:T(8,128)} %param.19) | copy-start | bytes 772
  756.6 283.5 %all-reduce.13.cloned.1.call-start = ((), (), s32[]{:S(2)}) async-start(), calls=%async_computation.3 | async-start | bytes 393216 | tf_op jit(solution)/shard_map/psum | solution.py:93
  792.8 49.8 %collective-permute-start.1 = (bf16[64,1]{1,0:T(8,128)(2,1)}, bf16[64,1]{1,0:T(8,128)(2,1)}, u32[]{:S(2)}, u32[]{:S(2)}) collective-permute-start(bf16[64,1]{1,0:T(8,128)(2,1)} %slice.144), channel_id=1, source_target_pairs={{0,8},{8,16},{16,24},{24,32},{32,40},{40,48},{48,56},{56,64},{64,7... | collective-permute-start | bytes 392 | tf_op jit(solution)/shard_map/ppermute | solution.py:14
  832.7 5.8 collective-permute-start
  835.7 2.8 copy-start.13
  835.7 2.8 copy-start.14
  840.5 2.1 copy-start.2
  840.5 2.1 copy-start.10
  845.1 196.6 %copy-start.4 = (f32[64,2048]{1,0:T(8,128)S(1)}, f32[64,2048]{1,0:T(8,128)}, u32[]{:S(2)}) copy-start(f32[64,2048]{1,0:T(8,128)} %all-reduce.11.cloned.1.call-done) | copy-start | bytes 1572868
Sparse Core Ops, SparseCore 0:
  10.1 47.9 all-gather.2
  281.1 265.3 all-reduce.8
  756.7 74.5 all-reduce.10
  850.1 189.9 all-reduce.12
where the time goes:
time: 1060 us; the launch traced here: 1050 us
  waiting for transfers between devices  395 us (37%)
  blocking collectives  364 us (34%)
  other arithmetic  130 us (12%)
  local copies, waits for them, and re-layouts  52.3 us (5%)
  starting transfers between devices  51.6 us (5%)
  matrix products  39.4 us (4%)
  between operations  17.7 us (2%)
    psum x1, waiting for transfers between devices, local(): lax.psum(jnp.dot(sketch_rows.T, sketch_rows, precision=precise), ('tm', '...  262 us
    unnamed x1, blocking collectives  141 us
    psum x1, blocking collectives, local(): lax.psum((jnp.dot(error, hidden.T, precision=precise), jnp.sum(squared, a...  129 us
    another operation x14, other arithmetic, orthonormal(): lower = jnp.linalg.cholesky(gram)  82.2 us
    all_gather x1, waiting for transfers between devices, local(): test_full = lax.all_gather(test_matrix, 'region', axis=1, tiled=True)  50.1 us
    unnamed x16, starting transfers between devices  47 us
    psum x1, waiting for transfers between devices, local(): lax.psum((jnp.dot(error, hidden.T, precision=precise), jnp.sum(squared, a...  45.1 us
    all_gather x1, blocking collectives, local(): lax.all_gather(loading_rows, 'tm', axis=0, tiled=True)  43.1 us
  transfers between devices with their start and end apart: 22, of which 4 were waited for; matrix products, arithmetic and copies ran while one was open for 1% of the time, Pallas kernels for 0%

commit v1 on v0

--- a/solution.py
+++ b/solution.py
@@ -6,6 +6,11 @@
 BLOCK = 128
 precise = lax.Precision.HIGHEST
 epsilon = 1e-05
+
+
+def gather_over(x, axis, dim):
+    outgoing = jnp.stack([x] * lax.axis_size(axis))
+    return jnp.concatenate(lax.all_to_all(outgoing, axis, 0, 0), axis=dim)
 
 
 def from_behind(block, axis, distance):
@@ -71,10 +76,7 @@
         jnp.bfloat16
     )
     latent_part = lax.dot_general(
-        lax.all_gather(loading_rows, "tm", axis=0, tiled=True),
-        activity,
-        contract,
-        preferred_element_type=jnp.float32,
+        gather_over(loading_rows, "tm", 0), activity, contract, preferred_element_type=jnp.float32
     )
     signal_part = lax.dot_general(
         region_feed, activity, contract, preferred_element_type=jnp.float32

time: 1060 us -> 999 us (0.942)
  blocking collectives: 364 us -> 323 us
  local copies, waits for them, and re-layouts: 52.3 us -> 30.1 us
    all_gather x1 -> x0, blocking collectives: 43.1 us -> none  [local(): lax.all_gather(loading_rows, 'tm', axis=0, tiled=True)]
    unnamed x40 -> x29, local copies, waits for them, and re-layouts: 29.9 us -> 9.25 us
  transfers between devices with their start and end apart: 22 -> 23, of which waited for: 4 -> 5; matrix products, arithmetic and copies ran while one was open for 1% -> 2% of each run, Pallas kernels for 0% -> 0%
where the time goes in v1:
time: 999 us; the launch traced here: 994 us
  waiting for transfers between devices  403 us (40%)
  blocking collectives  323 us (32%)
  other arithmetic  128 us (13%)
  starting transfers between devices  55.9 us (6%)
  matrix products  36.4 us (4%)
  local copies, waits for them, and re-layouts  30.1 us (3%)
  between operations  17.7 us (2%)
    psum x1, waiting for transfers between devices, local(): lax.psum(jnp.dot(sketch_rows.T, sketch_rows, precision=precise), ('tm', '...  265 us
    unnamed x1, blocking collectives  141 us
    psum x1, blocking collectives, local(): lax.psum((jnp.dot(error, hidden.T, precision=precise), jnp.sum(squared, a...  129 us
    another operation x14, other arithmetic, orthonormal(): lower = jnp.linalg.cholesky(gram)  80.9 us
    all_gather x1, waiting for transfers between devices, local(): test_full = lax.all_gather(test_matrix, 'region', axis=1, tiled=True)  50.1 us
    psum x1, waiting for transfers between devices, local(): lax.psum((jnp.dot(error, hidden.T, precision=precise), jnp.sum(squared, a...  45.5 us
    unnamed x16, starting transfers between devices  45.5 us
    another operation x3, other arithmetic, orthonormal(): return jax.scipy.linalg.solve_triangular(lower, sketch.T, lower=True).T  42.5 us
  transfers between devices with their start and end apart: 23, of which 5 were waited for; matrix products, arithmetic and copies ran while one was open for 2% of the time, Pallas kernels for 0%

profile of v1, /device:TPU:8, one launch (start us, length us, event | category | flops | bytes accessed | tf_op | source)
XLA Modules:
  0.0 993.7 jit_solution(606710493597999385)
XLA Ops:
  8.0 50.1 %all-gather.2.cloned.1.call-done = bf16[2048,512]{0,1:T(8,128)(2,1)} async-done(((bf16[2048,64]{0,1:T(8,128)(2,1)}), bf16[2048,512]{0,1:T(8,128)(2,1)}) %all-gather.2.cloned.1.call-update) | async-done | bytes 2097168 | tf_op jit(solution)/shard_map/all_gather | solution.py:67
  58.1 4.4 fusion.72
  62.4 140.5 %fusion = f32[16,512]{1,0:T(8,128)S(1)} fusion(f32[768,512]{1,0:T(8,128)S(1)} %fusion.72), kind=kCustom, calls=%all-reduce-scatter | all-reduce-scatter fusion | flops 524289 | bytes 1607680
  210.8 11.6 %collective-permute-start.11 = (f32[16,512]{1,0:T(8,128)S(1)}, f32[16,512]{1,0:T(8,128)S(1)}, u32[]{:S(2)}, u32[]{:S(2)}) collective-permute-start(f32[16,512]{1,0:T(8,128)S(1)} %fusion), channel_id=1, source_target_pairs={{0,80},{8,88},{16,96},{24,104},{32,112},{40,120},{48,128},{56,136}... | collective-permute-start | bytes 98312
  222.4 1.9 collective-permute-start.10
  224.4 5.7 collective-permute-start.9
  231.5 3.8 collective-permute-start.7
  235.4 3.5 collective-permute-start.6
  238.9 2.7 collective-permute-start.5
  241.7 2.7 collective-permute-start.4
  244.4 2.1 collective-permute-start.3
  246.5 2.2 collective-permute-start.2
  251.4 2.2 concatenate.21
  253.6 2.1 fusion.49
  257.1 265.4 %all-reduce.9.cloned.1.call-done = f32[512,512]{0,1:T(8,128)} async-done(((f32[512,512]{0,1:T(8,128)}), f32[512,512]{0,1:T(8,128)}) %all-reduce.9.cloned.1.call-update) | async-done | bytes 1048592 | tf_op jit(solution)/shard_map/psum | solution.py:74
  522.5 1.6 copy.25
  525.6 11.7 %cholesky.104 = f32[128,128]{1,0:T(8,128)S(1)} custom-call(f32[128,128]{1,0:T(8,128)S(1)} %cholesky.266), custom_call_target="Cholesky" | custom-call | tf_op jit(solution)/shard_map/jit(cholesky)/cholesky | solution.py:23
  537.3 9.8 custom-call.31
  549.7 11.7 %cholesky.217 = f32[128,128]{1,0:T(8,128)S(1)} custom-call(f32[128,128]{1,0:T(8,128)S(1)} %cholesky.270), custom_call_target="Cholesky" | custom-call | tf_op jit(solution)/shard_map/jit(cholesky)/cholesky | solution.py:23
  562.1 10.3 %custom-call.32 = f32[1,128,128]{1,2,0:T(8,128)S(1)} custom-call(f32[1,128,128]{2,1,0:T(8,128)S(1)} %get-tuple-element.31), custom_call_target="InvertDiagBlocksLowerTriangular" | custom-call | tf_op jit(solution)/shard_map/jit(cholesky)/cholesky | solution.py:23
  573.3 1.6 convolution_subtract_fusion.1
  574.9 11.7 %cholesky.238 = f32[128,128]{1,0:T(8,128)S(1)} custom-call(f32[128,128]{1,0:T(8,128)S(1)} %cholesky.275), custom_call_target="Cholesky" | custom-call | tf_op jit(solution)/shard_map/jit(cholesky)/cholesky | solution.py:23
  587.9 9.8 custom-call.33
  600.0 11.9 %cholesky.255 = f32[128,128]{1,0:T(8,128)S(1)} custom-call(f32[128,128]{1,0:T(8,128)S(1)} %convolution_subtract_fusion.2), custom_call_target="Cholesky" | custom-call | tf_op jit(solution)/shard_map/jit(cholesky)/cholesky | solution.py:23
  616.3 2.3 select_select_fusion
  618.6 13.7 %while.1 = (s32[]{:T(128)}, f32[512,512]{1,0:T(8,128)}, s32[4,2]{0,1:T(2,128)S(1)}, f32[4,128,128]{2,1,0:T(8,128)}, s32[]{:T(128)}) while((s32[]{:T(128)}, f32[512,512]{1,0:T(8,128)}, s32[4,2]{0,1:T(2,128)S(1)}, f32[4,128,128]{2,1,0:T(8,128)}, s32[]{:T(128)}) %tuple.34), condition=%wide.while_cond, body=%wide.while_body.sunk | while | flops 2 | bytes 132205 | solution.py:24
  619.2 2.8 bitcast_dynamic-update-slice_fusion.2
  622.7 2.8 bitcast_dynamic-update-slice_fusion.2
  626.1 2.8 bitcast_dynamic-update-slice_fusion.2
  629.6 2.8 bitcast_dynamic-update-slice_fusion.2
  632.3 40.1 %custom-call.34 = f32[4,128,128]{1,2,0:T(8,128)S(1)} custom-call(f32[4,128,128]{2,1,0:T(8,128)} %get-tuple-element.10), custom_call_target="InvertDiagBlocksLowerTriangular" | custom-call | tf_op jit(solution)/shard_map/jit(_solve_triangular)/triangular_solve | solution.py:24
  680.5 6.5 all-to-all-start
  687.0 2.2 fusion.25
  689.2 7.7 all-to-all-done
  698.8 2.4 fusion.73
  701.3 37.6 %all-reduce.14 = bf16[64,2048]{1,0:T(8,128)(2,1)S(1)} all-reduce(f32[64,2048]{1,0:T(8,128)} %fusion.25), channel_id=1, replica_groups=mesh['tm'=64,'region'=8] {'region'}, use_global_device_ids=true, to_apply=%region_11.12 | all-reduce | flops 131072 | bytes 786432 | tf_op jit(solution)/shard_map/psum | solution.py:84
  739.6 1.9 collective-permute-start.1
  741.5 33.8 %all-reduce.11.cloned.1.call-done = f32[64,2048]{1,0:T(8,128)} async-done(((f32[64,2048]{1,0:T(8,128)}), f32[64,2048]{1,0:T(8,128)}) %all-reduce.11.cloned.1.call-update) | async-done | bytes 524304 | tf_op jit(solution)/shard_map/psum | solution.py:84
  776.7 1.9 collective-permute-start
  779.5 3.0 copy.26
  782.5 1.9 multiply_reduce_fusion.2
  784.5 2.1 fusion.11
  786.6 2.5 multiply_reduce_fusion
  789.1 4.8 fusion.74
  793.9 129.4 %all-reduce.3 = (f32[64]{0:T(128)S(1)}, f32[768]{0:T(1024)S(1)}) all-reduce(f32[64]{0:T(128)S(1)} %get-tuple-element.38, f32[768]{0:T(1024)S(1)} %get-tuple-element.11), channel_id=1, replica_groups=mesh['tm'=64,'region'=8] {'tm'}, use_global_device_ids=true, to_apply=%region_18.19 | all-reduce | flops 832 | bytes 6656 | tf_op jit(solution)/shard_map/psum | solution.py:95
  923.4 15.0 %psum.52 = f32[2048]{0:T(1024)S(1)} all-reduce(f32[2048]{0:T(1024)S(1)} %get-tuple-element.12), channel_id=1, replica_groups=mesh['tm'=64,'region'=8] {'region'}, use_global_device_ids=true, to_apply=%region_13.14 | all-reduce | flops 2048 | bytes 16384 | tf_op jit(solution)/shard_map/psum | solution.py:103
  939.0 45.5 %all-reduce.13.cloned.1.call-done = f32[768,64]{0,1:T(8,128)} async-done(((f32[768,64]{0,1:T(8,128)}), f32[768,64]{0,1:T(8,128)}) %all-reduce.13.cloned.1.call-update) | async-done | bytes 196624 | tf_op jit(solution)/shard_map/psum | solution.py:95
  984.4 1.7 rsqrt_multiply_fusion
  (110 shorter events, 41.4 us)
Async XLA Ops:
  7.2 672.2 %copy-start = (f32[512,64]{0,1:T(8,128)S(1)}, f32[512,64]{0,1:T(8,128)}, u32[]{:S(2)}) copy-start(f32[512,64]{0,1:T(8,128)} %param.12) | copy-start | bytes 393220
  7.2 50.9 %all-gather.2.cloned.1.call-start = ((), (), s32[]{:S(2)}) async-start(), calls=%async_computation.1 | async-start | bytes 2359296 | tf_op jit(solution)/shard_map/all_gather | solution.py:67
  7.9 240.8 %copy-start.6 = (bf16[768,8]{0,1:T(8,128)(2,1)S(1)}, bf16[768,8]{0,1:T(8,128)(2,1)}, u32[]{:S(2)}) copy-start(bf16[768,8]{0,1:T(8,128)(2,1)} %param.16) | copy-start | bytes 36868
  7.9 243.4 %copy-start.10 = (s32[48]{0:T(128)S(1)}, s32[48]{0:T(128)}, u32[]{:S(2)}) copy-start(s32[48]{0:T(128)} %param.18) | copy-start | bytes 580
  7.9 514.6 %all-reduce.9.cloned.1.call-start = ((), (), s32[]{:S(2)}) async-start(), calls=%async_computation.2 | async-start | bytes 2097152 | tf_op jit(solution)/shard_map/psum | solution.py:74
  203.0 6.5 collective-permute-start.17
  204.3 6.5 collective-permute-start.16
  205.6 16.8 %collective-permute-start.15 = (f32[16,512]{1,0:T(8,128)S(1)}, f32[16,512]{1,0:T(8,128)S(1)}, u32[]{:S(2)}, u32[]{:S(2)}) collective-permute-start(f32[16,512]{1,0:T(8,128)S(1)} %fusion), channel_id=1, source_target_pairs={{0,112},{8,120},{16,128},{24,136},{32,144},{40,152},{48,160},{56,1... | collective-permute-start | bytes 98312
  206.9 17.4 %collective-permute-start.14 = (f32[16,512]{1,0:T(8,128)S(1)}, f32[16,512]{1,0:T(8,128)S(1)}, u32[]{:S(2)}, u32[]{:S(2)}) collective-permute-start(f32[16,512]{1,0:T(8,128)S(1)} %fusion), channel_id=1, source_target_pairs={{0,104},{8,112},{16,120},{24,128},{32,136},{40,144},{48,152},{56,1... | collective-permute-start | bytes 98312
  208.2 21.8 %collective-permute-start.13 = (f32[16,512]{1,0:T(8,128)S(1)}, f32[16,512]{1,0:T(8,128)S(1)}, u32[]{:S(2)}, u32[]{:S(2)}) collective-permute-start(f32[16,512]{1,0:T(8,128)S(1)} %fusion), channel_id=1, source_target_pairs={{0,96},{8,104},{16,112},{24,120},{32,128},{40,136},{48,144},{56,15... | collective-permute-start | bytes 98312
  209.5 22.0 %collective-permute-start.12 = (f32[16,512]{1,0:T(8,128)S(1)}, f32[16,512]{1,0:T(8,128)S(1)}, u32[]{:S(2)}, u32[]{:S(2)}) collective-permute-start(f32[16,512]{1,0:T(8,128)S(1)} %fusion), channel_id=1, source_target_pairs={{0,88},{8,96},{16,104},{24,112},{32,120},{40,128},{48,136},{56,144... | collective-permute-start | bytes 98312
  210.8 24.5 %collective-permute-start.11 = (f32[16,512]{1,0:T(8,128)S(1)}, f32[16,512]{1,0:T(8,128)S(1)}, u32[]{:S(2)}, u32[]{:S(2)}) collective-permute-start(f32[16,512]{1,0:T(8,128)S(1)} %fusion), channel_id=1, source_target_pairs={{0,80},{8,88},{16,96},{24,104},{32,112},{40,120},{48,128},{56,136}... | collective-permute-start | bytes 98312
  222.4 16.5 %collective-permute-start.10 = (f32[16,512]{1,0:T(8,128)S(1)}, f32[16,512]{1,0:T(8,128)S(1)}, u32[]{:S(2)}, u32[]{:S(2)}) collective-permute-start(f32[16,512]{1,0:T(8,128)S(1)} %fusion), channel_id=1, source_target_pairs={{0,72},{8,80},{16,88},{24,96},{32,104},{40,112},{48,120},{56,128},... | collective-permute-start | bytes 98312
  224.4 17.3 %collective-permute-start.9 = (f32[16,512]{1,0:T(8,128)S(1)}, f32[16,512]{1,0:T(8,128)S(1)}, u32[]{:S(2)}, u32[]{:S(2)}) collective-permute-start(f32[16,512]{1,0:T(8,128)S(1)} %fusion), channel_id=1, source_target_pairs={{0,64},{8,72},{16,80},{24,88},{32,96},{40,104},{48,112},{56,120},{... | collective-permute-start | bytes 98312
  230.0 14.3 %collective-permute-start.8 = (f32[16,512]{1,0:T(8,128)S(1)}, f32[16,512]{1,0:T(8,128)S(1)}, u32[]{:S(2)}, u32[]{:S(2)}) collective-permute-start(f32[16,512]{1,0:T(8,128)S(1)} %fusion), channel_id=1, source_target_pairs={{0,56},{8,64},{16,72},{24,80},{32,88},{40,96},{48,104},{56,112},{6... | collective-permute-start | bytes 98312
  231.5 15.0 %collective-permute-start.7 = (f32[16,512]{1,0:T(8,128)S(1)}, f32[16,512]{1,0:T(8,128)S(1)}, u32[]{:S(2)}, u32[]{:S(2)}) collective-permute-start(f32[16,512]{1,0:T(8,128)S(1)} %fusion), channel_id=1, source_target_pairs={{0,48},{8,56},{16,64},{24,72},{32,80},{40,88},{48,96},{56,104},{64... | collective-permute-start | bytes 98312
  235.4 16.0 %collective-permute-start.6 = (f32[16,512]{1,0:T(8,128)S(1)}, f32[16,512]{1,0:T(8,128)S(1)}, u32[]{:S(2)}, u32[]{:S(2)}) collective-permute-start(f32[16,512]{1,0:T(8,128)S(1)} %fusion), channel_id=1, source_target_pairs={{0,40},{8,48},{16,56},{24,64},{32,72},{40,80},{48,88},{56,96},{64,... | collective-permute-start | bytes 98312
  238.9 12.5 %collective-permute-start.5 = (f32[16,512]{1,0:T(8,128)S(1)}, f32[16,512]{1,0:T(8,128)S(1)}, u32[]{:S(2)}, u32[]{:S(2)}) collective-permute-start(f32[16,512]{1,0:T(8,128)S(1)} %fusion), channel_id=1, source_target_pairs={{0,32},{8,40},{16,48},{24,56},{32,64},{40,72},{48,80},{56,88},{64,... | collective-permute-start | bytes 98312
  241.7 9.7 collective-permute-start.4
  244.4 7.0 collective-permute-start.3
  246.5 4.9 collective-permute-start.2
  525.6 46.8 %copy-start.3 = (f32[512,512]{1,0:T(8,128)}, f32[512,512]{1,0:T(8,128)S(1)}, u32[]{:S(2)}) copy-start(f32[512,512]{1,0:T(8,128)S(1)} %fusion.3) | copy-start | bytes 3145732
  573.3 113.7 %copy-start.1 = (bf16[768,2048]{1,0:T(8,128)(2,1)S(1)}, bf16[768,2048]{1,0:T(8,128)(2,1)}, u32[]{:S(2)}) copy-start(bf16[768,2048]{1,0:T(8,128)(2,1)} %param.10) | copy-start | bytes 9437188
  680.5 16.5 %all-to-all-start = ((bf16[64,2,384]{2,1,0:T(2,128)(2,1)}), bf16[64,2,384]{2,1,0:T(2,128)(2,1)}, u32[]{:S(2)}, u32[]{:S(2)}) async-start(bf16[64,2,384]{2,1,0:T(2,128)(2,1)} %reshape.115), calls=%async_computation | async-start | bytes 196608 | tf_op jit(solution)/shard_map/all_to_all | solution.py:13
  686.9 88.3 %all-reduce.11.cloned.1.call-start = ((), (), s32[]{:S(2)}) async-start(), calls=%async_computation.3 | async-start | bytes 1048576 | tf_op jit(solution)/shard_map/psum | solution.py:84
  689.2 89.4 %copy-start.9 = (s32[8,8]{1,0:T(8,128)S(1)}, s32[8,8]{1,0:T(8,128)}, u32[]{:S(2)}) copy-start(s32[8,8]{1,0:T(8,128)} %param.19) | copy-start | bytes 772
  701.2 283.2 %all-reduce.13.cloned.1.call-start = ((), (), s32[]{:S(2)}) async-start(), calls=%async_computation.4 | async-start | bytes 393216 | tf_op jit(solution)/shard_map/psum | solution.py:95
  739.6 46.9 %collective-permute-start.1 = (bf16[64,1]{1,0:T(8,128)(2,1)}, bf16[64,1]{1,0:T(8,128)(2,1)}, u32[]{:S(2)}, u32[]{:S(2)}) collective-permute-start(bf16[64,1]{1,0:T(8,128)(2,1)} %slice.144), channel_id=1, source_target_pairs={{0,8},{8,16},{16,24},{24,32},{32,40},{40,48},{48,56},{56,64},{64,7... | collective-permute-start | bytes 392 | tf_op jit(solution)/shard_map/ppermute | solution.py:19
  776.7 5.8 collective-permute-start
  779.5 3.0 copy-start.7
  779.5 3.0 copy-start.8
  784.4 2.1 copy-start.2
  784.4 2.1 copy-start.5
  789.1 197.1 %copy-start.4 = (f32[64,2048]{1,0:T(8,128)S(1)}, f32[64,2048]{1,0:T(8,128)}, u32[]{:S(2)}) copy-start(f32[64,2048]{1,0:T(8,128)} %all-reduce.11.cloned.1.call-done) | copy-start | bytes 1572868
Sparse Core Ops, SparseCore 0:
  10.1 47.9 all-gather.1
  255.8 266.6 all-reduce.8
  701.3 73.8 all-reduce.10
  794.0 190.3 all-reduce.12
